TPU v7x, 32 devices: a whole 2x2x4 slice. The times are simulated.
32 devices in a mesh: dp: 2 (over x), seq: 8 (over z, y), head: 2 (over core).
Axes of the slice: x: 2, y: 2, z: 4, core: 2. Of those that a mesh axis runs over, the one named last changes fastest.
Arguments:
- queries: bfloat16 [3072, 2048], P(('dp', 'seq'), 'head'), parts along dimension 0, may hold values from -6 to 6
- keys: bfloat16 [3072, 2048], P(('dp', 'seq'), 'head'), parts along dimension 0, may hold values from -6 to 6
- values: bfloat16 [3072, 2048], P(('dp', 'seq'), 'head'), parts along dimension 0, may hold values from -6 to 6
- segments: int32 [3072], P(('dp', 'seq')), parts along dimension 0, may hold values from 0 to 2, never falling along the last dimension, each value on 1 to 768 neighbouring positions
- hidden_in: bfloat16 [3072, 2048], P(('dp', 'seq', 'head')), parts along dimension 0, may hold values from -6 to 6
- attn_gain: float32 [2048], P('head'), may hold values from 0.25 to 1.75
- out_proj: bfloat16 [2048, 2048], P('head', 'seq'), may hold values from -0.125 to 0.125
- moe_gain: float32 [2048], replicated, may hold values from 0.1 to 1.9
- route_ids: int32 [3072, 8], P(('dp', 'seq', 'head')), parts along dimension 0, may hold values from 0 to 15, all different within a row; in each aligned block of 96 rows (0 to 95, 96 to 191, ...) at most 64 rows name the same one
- route_w: float32 [3072, 8], P(('dp', 'seq', 'head')), parts along dimension 0, may hold values from 0.02 to 0.5
- w_gate: bfloat16 [16, 2048, 768], P(('seq', 'head')), may hold values from -0.125 to 0.125
- w_up: bfloat16 [16, 2048, 768], P(('seq', 'head')), may hold values from -0.125 to 0.125
- w_down: bfloat16 [16, 768, 2048], P(('seq', 'head')), may hold values from -0.625 to 0.625
Outputs:
- block_out: bfloat16 [3072, 2048], P(('dp', 'seq', 'head')), parts along dimension 0
There are 2 independent parts, one for each index of `dp`. A program takes and returns all parts, laid end to end along the dimension named above; an argument that names none is the same for every part. Nothing has to cross between parts.
Inputs may be any that keep to these rules, and one draw needn't show every extreme that they name: `route_ids`: each row names 8 different experts. In the 96 rows of one device no expert is named more than 64 times; in some device's rows some expert is named exactly 64 times. `segments`: ids of 3 packed documents, never falling, every document at least one token, the longest exactly 768 tokens.
All inputs are finite; a program needn't handle non-finite values.
Results may differ from a plain program's by a relative error of at most 0.0065.
Values may be sent and summed in bfloat16 or wider, within the bound.
A program may use at most 128 MiB of HBM per device.

v0:
```python
import jax
import jax.numpy as jnp
from jax import lax
from jax.sharding import PartitionSpec as P

D = 2048
DK = 128
TOPK = 8


epsilon = 1e-06


def carried_in(part, axis, combine, identity):
    place = lax.axis_index(axis)
    gathered = jax.tree.map(lambda a: lax.all_gather(a, axis), part)
    state = jax.tree.map(lambda a, e: jnp.zeros_like(a) + jnp.asarray(e, a.dtype), part, identity)

    def one(turn, state):
        return combine(
            state, jax.tree.map(lambda a: lax.dynamic_index_in_dim(a, turn, 0, False), gathered)
        )

    return lax.fori_loop(0, place, one, state)


def combine(earlier, later):
    first_one, last_one, state_one = earlier
    first_two, last_two, state_two = later
    keep_state = (first_two >= last_one) & (last_two <= last_one)
    merged = state_two + jnp.where(keep_state, state_one, jnp.zeros_like(state_one))
    return (jnp.minimum(first_one, first_two), jnp.maximum(last_one, last_two), merged)


def local(
    queries,
    keys,
    values,
    segments,
    hidden_in,
    attn_gain,
    out_proj,
    moe_gain,
    route_ids,
    route_w,
    w_gate,
    w_up,
    w_down,
):
    tok_rows = queries.shape[0]
    heads_here = attn_gain.shape[0] // DK
    query_rows = queries.reshape(tok_rows, heads_here, DK)
    key_rows = keys.reshape(tok_rows, heads_here, DK)
    value_rows = values.reshape(tok_rows, heads_here, DK)
    position = jnp.arange(tok_rows)
    causal = position[:, None] >= position[None, :]
    same_doc = (segments[:, None] == segments[None, :]) & causal
    scores = jnp.einsum("thd,shd->hts", query_rows, key_rows, preferred_element_type=jnp.float32)
    scores = jnp.where(same_doc[None], scores, 0.0)
    local_part = jnp.einsum(
        "hts,shd->thd", scores, value_rows.astype(jnp.float32), precision=lax.Precision.HIGHEST
    )
    tail_mask = (segments == segments[-1])[:, None, None]
    tail_keys = jnp.where(tail_mask, key_rows, jnp.zeros_like(key_rows))
    own_state = jnp.einsum(
        "thd,the->hde", tail_keys, value_rows, preferred_element_type=jnp.float32
    )
    first_seg = segments[0].astype(jnp.float32)
    last_seg = segments[-1].astype(jnp.float32)
    identity = (jnp.float32(1000000000.0), jnp.float32(-1.0), jnp.zeros_like(own_state))
    prefix_first, prefix_last, prefix_state = carried_in(
        (first_seg, last_seg, own_state), "seq", combine, identity
    )
    continued = (segments.astype(jnp.float32) == prefix_last)[:, None, None]
    carried_part = jnp.einsum(
        "thd,hde->the",
        query_rows.astype(jnp.float32),
        prefix_state,
        precision=lax.Precision.HIGHEST,
    )
    attn_raw = local_part + jnp.where(continued, carried_part, 0.0)
    mean_square = jnp.mean(attn_raw * attn_raw, axis=-1, keepdims=True)
    attended = attn_raw * lax.rsqrt(mean_square + epsilon) * attn_gain.reshape(heads_here, DK)
    attended = attended.astype(jnp.bfloat16).reshape(tok_rows, heads_here * DK)
    partial_out = jnp.dot(
        attended,
        lax.all_gather(out_proj, "seq", axis=1, tiled=True),
        preferred_element_type=jnp.float32,
    )
    attn_out = lax.psum_scatter(partial_out, "head", scatter_dimension=0, tiled=True)
    mid_wide = (hidden_in.astype(jnp.float32) + attn_out).astype(jnp.bfloat16).astype(jnp.float32)
    mid_square = jnp.mean(mid_wide * mid_wide, axis=-1, keepdims=True)
    normed = (mid_wide * lax.rsqrt(mid_square + epsilon) * moe_gain).astype(jnp.bfloat16)
    weights = route_w / jnp.sum(route_w, axis=1, keepdims=True)
    tok_dev = route_ids.shape[0]
    experts = lax.axis_size("seq") * lax.axis_size("head")
    capacity = 4 * tok_dev * TOPK // (3 * experts)
    flat_ids = route_ids.reshape(-1)
    labels = jnp.arange(experts, dtype=jnp.int32)
    onehot = (flat_ids[:, None] == labels[None, :]).astype(jnp.int32)
    before = jnp.cumsum(onehot, axis=0) - onehot
    slot_index = jnp.sum(before * onehot, axis=1)
    destination = (flat_ids * capacity + slot_index).reshape(tok_dev, TOPK)
    places = jnp.arange(experts * capacity, dtype=jnp.int32)
    selector = jnp.any(destination[None, :, :] == places[:, None, None], axis=2).astype(
        jnp.bfloat16
    )
    outgoing = jnp.dot(selector, normed, preferred_element_type=jnp.float32).astype(jnp.bfloat16)
    outgoing = outgoing.reshape(experts, capacity, D)
    arrived = lax.all_to_all(outgoing, ("seq", "head"), split_axis=0, concat_axis=0, tiled=True)
    row_shape = arrived.shape
    flat_rows = arrived.reshape(-1, row_shape[-1])
    gate_part = jnp.dot(flat_rows, w_gate[0], preferred_element_type=jnp.float32)
    up_part = jnp.dot(flat_rows, w_up[0], preferred_element_type=jnp.float32)
    inner = (jax.nn.silu(gate_part) * up_part).astype(jnp.bfloat16)
    answer = jnp.dot(inner, w_down[0], preferred_element_type=jnp.float32).astype(jnp.bfloat16)
    returned = lax.all_to_all(
        answer.reshape(row_shape), ("seq", "head"), split_axis=0, concat_axis=0, tiled=True
    )
    flat_out = returned.reshape(experts * capacity, D)
    picked = jnp.take(flat_out, destination.reshape(-1), axis=0).reshape(tok_dev, TOPK, D)
    mixture = jnp.sum(weights[:, :, None] * picked.astype(jnp.float32), axis=1)
    return (mid_wide + mixture).astype(jnp.bfloat16)


def solution(mesh):
    return jax.shard_map(
        local,
        mesh=mesh,
        in_specs=(
            P(("dp", "seq"), "head"),
            P(("dp", "seq"), "head"),
            P(("dp", "seq"), "head"),
            P(("dp", "seq")),
            P(("dp", "seq", "head"), None),
            P("head"),
            P("head", "seq"),
            P(),
            P(("dp", "seq", "head"), None),
            P(("dp", "seq", "head"), None),
            P(("seq", "head"), None, None),
            P(("seq", "head"), None, None),
            P(("seq", "head"), None, None),
        ),
        out_specs=P(("dp", "seq", "head"), None),
        check_vma=False,
    )
```

profile of v0, /device:TPU:13, one launch (start us, length us, event | category | flops | bytes accessed | tf_op | source)
XLA Modules:
  0.0 416.1 jit_solution(3173747557035355574)
XLA Ops:
  6.5 0.0 copy-start
  6.5 0.0 all-gather.6.cloned.1.call-start
  6.5 1.4 slice.13
  7.9 1.3 broadcast_compare_fusion
  9.3 2.3 fusion.30
  11.6 0.0 all-gather.6.cloned.1.call-update
  11.6 0.0 all-gather.4.cloned.1.call-start
  11.7 0.7 all-gather.4.cloned.1.call-update
  12.4 0.0 reduce-scatter.2.cloned.1.call-start
  13.1 1.2 dynamic-slice
  14.3 1.4 convert_dynamic-update-slice_fusion
  15.7 0.8 dynamic-update-slice
  16.5 12.7 %all-reduce.2 = (f32[8]{0:T(128)S(1)}, f32[8]{0:T(128)S(1)}) all-reduce(f32[8]{0:T(128)S(1)} %dynamic-update-slice, f32[8]{0:T(128)S(1)} %convert_dynamic-update-slice_fusion), channel_id=1, replica_groups=mesh['dp'=2,'seq'=8,'head'=2] {'seq'}, use_global_device_ids=true, to_apply=%add | all-reduce | flops 16 | bytes 128
  29.2 1.5 fusion.47
  30.7 2.7 fusion.33
  33.4 50.6 %all-gather.6.cloned.1.call-done = f32[64,128,128]{2,1,0:T(8,128)} async-done(((f32[8,128,128]{2,1,0:T(8,128)}), f32[64,128,128]{2,1,0:T(8,128)}) %all-gather.6.cloned.1.call-update) | async-done | bytes 4194320 | tf_op jit(solution)/shard_map/all_gather | solution.py:16
  84.0 0.8 broadcast.123
  84.8 15.2 %while.14 = (s32[]{:T(128)}, f32[]{:T(128)}, f32[8,128,128]{2,1,0:T(8,128)}, s32[]{:T(128)}, f32[8]{0:T(128)S(1)}, /*index=5*/f32[8,8,128,128]{3,2,1,0:T(8,128)}, f32[8]{0:T(128)S(1)}, s32[]{:T(128)}, s32[]{:T(128)}, s32[]{:T(128)}) while((s32[]{:T(128)}, f32[]{:T(128)}, f32[8,128,128]{2,1,0:T(8,128)}, s32[]{:T(128)}, f32[8]{0:T(128)S(1)}, ...), condition=%wide.region_1.2_spmd, body=%wide.region_0.1_spmd.sunk | while | flops 262153 | bytes 1573061 | solution.py:24
  84.8 0.6 dynamic_slice.19
  86.0 0.6 dynamic_slice.20
  87.3 1.9 bitcast_add_fusion.2
  89.8 0.6 dynamic_slice.19
  91.1 0.6 dynamic_slice.20
  92.3 2.1 bitcast_add_fusion.2
  95.0 0.6 dynamic_slice.19
  96.2 0.6 dynamic_slice.20
  97.5 1.9 bitcast_add_fusion.2
  100.0 0.0 copy-start.5
  100.1 1.5 fusion.16
  101.6 3.3 multiply_reduce_fusion.1
  105.0 53.9 %all-gather.4.cloned.1.call-done = bf16[1024,2048]{1,0:T(8,128)(2,1)} async-done(((bf16[1024,256]{1,0:T(8,128)(2,1)}), bf16[1024,2048]{1,0:T(8,128)(2,1)}) %all-gather.4.cloned.1.call-update) | async-done | bytes 4194320 | tf_op jit(solution)/shard_map/all_gather | solution.py:87
  158.8 4.7 %fusion.27 = f32[192,2048]{1,0:T(8,128)} fusion(bf16[1024,2048]{1,0:T(8,128)(2,1)} %all-gather.4.cloned.1.call-done, f32[192,8,128]{2,0,1:T(8,128)} %get-tuple-element.87, f32[8,128]{1,0:T(8,128)S(1)} %bitcast.118, f32[192,8]{0,1:T(8,128)S(1)} %add_rsqrt_fusion), kind=kOutput, calls=%fused_computation.33 | convolution fusion | flops 805896192 | bytes 6563840 | tf_op jit(solution)/shard_map/dot_general | solution.py:85
  163.5 0.0 reduce-scatter.2.cloned.1.call-update
  163.5 0.1 copy.63
  163.6 0.1 eq.75
  163.7 0.1 reshape.160
  163.8 1.7 reduce-window.6
  165.5 0.3 slice_reduce_fusion
  165.8 0.1 fusion.50
  165.9 0.1 reduce_sum.52
  166.0 0.1 copy.66
  166.0 0.6 compare_and_fusion
  166.6 0.1 copy.68
  166.7 1.7 fusion.5
  168.4 6.4 %reduce-scatter.2.cloned.1.call-done = f32[96,2048]{1,0:T(8,128)} async-done(((f32[192,2048]{1,0:T(8,128)}), f32[96,2048]{1,0:T(8,128)}) %reduce-scatter.2.cloned.1.call-update) | async-done | bytes 786448 | tf_op jit(solution)/shard_map/reduce_scatter | solution.py:90
  174.7 1.4 fusion.19
  176.2 2.2 convolution_convert_fusion.1
  178.4 0.0 copy-start.6
  178.4 98.2 %all_to_all.10 = bf16[16,64,2048]{2,1,0:T(8,128)(2,1)S(1)} all-to-all(bf16[16,64,2048]{2,1,0:T(8,128)(2,1)S(1)} %bitcast.112), channel_id=1, replica_groups=mesh['dp'=2,'seq'=8,'head'=2] {'seq','head'}, dimensions={0} | all-to-all | bytes 8388608 | tf_op jit(solution)/shard_map/all_to_all | solution.py:110
  276.7 2.0 copy-done.1
  278.7 5.2 %fusion.1 = f32[1024,768]{1,0:T(8,128)} fusion(bf16[1024,2048]{1,0:T(8,128)(2,1)S(1)} %bitcast.114, bf16[1,2048,768]{2,1,0:T(8,128)(2,1)S(1)} %copy-done.6), kind=kOutput, calls=%fused_computation.7 | convolution fusion | flops 3221225472 | bytes 10485760 | tf_op jit(solution)/shard_map/dot_general | solution.py:114
  283.8 12.3 %convolution_convert_fusion = bf16[1024,2048]{1,0:T(8,128)(2,1)} fusion(bf16[1,768,2048]{2,1,0:T(8,128)(2,1)S(1)} %copy-done, f32[1024,768]{1,0:T(8,128)} %fusion.1, bf16[1024,2048]{1,0:T(8,128)(2,1)} %bitcast.115, bf16[1,2048,768]{2,1,0:T(8,128)(2,1)} %param.25), kind=kOutput, calls=%fused_computation.3 | convolution fusion | flops 6449266688 | bytes 17825792 | tf_op jit(solution)/shard_map/dot_general | solution.py:116
  296.1 5.3 %all-to-all-start.1 = ((bf16[16,64,2048]{2,1,0:T(8,128)(2,1)}), bf16[16,64,2048]{2,1,0:T(8,128)(2,1)}, u32[]{:S(2)}, u32[]{:S(2)}) async-start(bf16[16,64,2048]{2,1,0:T(8,128)(2,1)} %bitcast.113), calls=%async_computation.2 | async-start | bytes 8388608 | tf_op jit(solution)/shard_map/all_to_all | solution.py:117
  301.4 0.7 copy.69
  302.1 1.5 mul.96
  303.6 0.7 copy.67
  304.4 1.2 reduce_sum.50
  305.6 1.3 broadcast_divide_fusion
  306.9 1.4 copy.62
  308.3 0.7 fusion.52
  309.0 84.9 %all-to-all-done.1 = bf16[16,64,2048]{2,1,0:T(8,128)(2,1)} async-done(((bf16[16,64,2048]{2,1,0:T(8,128)(2,1)}), bf16[16,64,2048]{2,1,0:T(8,128)(2,1)}, u32[]{:S(2)}, u32[]{:S(2)}) %all-to-all-start.1) | async-done | bytes 4194336 | tf_op jit(solution)/shard_map/all_to_all | solution.py:117
  393.9 9.8 %gather_fusion = bf16[768,2048]{1,0:T(8,128)(2,1)} fusion(bf16[1024,2048]{1,0:T(8,128)(2,1)} %bitcast.17, s32[1024]{0:T(1024)S(1)} %pad_clamp_fusion), kind=kCustom, calls=%fused_computation | custom fusion | bytes 6294528 | tf_op jit(solution)/shard_map/jit(_take)/gather | solution.py:121
  403.7 5.0 %multiply_reduce_fusion = f32[96,2048]{1,0:T(8,128)S(1)} fusion(bf16[768,2048]{1,0:T(8,128)(2,1)} %gather_fusion, f32[96,8]{1,0:T(8,128)} %copy.62, pred[96,8]{1,0:T(8,128)(4,1)S(1)} %copy.67), kind=kLoop, calls=%fused_computation.2 | loop fusion | flops 6094848 | bytes 3936000 | tf_op jit(solution)/shard_map/reduce_sum | solution.py:122
  408.7 0.8 fusion.22
  (19 shorter events, 0.1 us)
Async XLA Ops:
  6.5 277.3 %copy-start = (bf16[1,768,2048]{2,1,0:T(8,128)(2,1)S(1)}, bf16[1,768,2048]{2,1,0:T(8,128)(2,1)}, u32[]{:S(2)}) copy-start(bf16[1,768,2048]{2,1,0:T(8,128)(2,1)} %param.27) | copy-start | bytes 9437188
  6.5 77.4 %all-gather.6.cloned.1.call-start = ((), (), s32[]{:S(2)}) async-start(), calls=%async_computation.5 | async-start | bytes 4718592 | tf_op jit(solution)/shard_map/all_gather | solution.py:16
  11.6 147.2 %all-gather.4.cloned.1.call-start = ((), (), s32[]{:S(2)}) async-start(), calls=%async_computation.3 | async-start | bytes 4718592 | tf_op jit(solution)/shard_map/all_gather | solution.py:87
  12.4 162.3 %reduce-scatter.2.cloned.1.call-start = ((), (), s32[]{:S(2)}) async-start(), calls=%async_computation.4 | async-start | bytes 2359296 | tf_op jit(solution)/shard_map/reduce_scatter | solution.py:90
  84.8 15.3 %copy-start.4 = (s32[192]{0:T(256)S(1)}, s32[192]{0:T(256)}, u32[]{:S(2)}) copy-start(s32[192]{0:T(256)} %param.18) | copy-start | bytes 2308
  84.8 15.3 %copy-start.2 = (bf16[192,1024]{1,0:T(8,128)(2,1)S(1)}, bf16[192,1024]{1,0:T(8,128)(2,1)}, u32[]{:S(2)}) copy-start(bf16[192,1024]{1,0:T(8,128)(2,1)} %param.15) | copy-start | bytes 1179652
  100.0 58.8 %copy-start.5 = (f32[1024]{0:T(1024)S(1)}, f32[1024]{0:T(1024)}, u32[]{:S(2)}) copy-start(f32[1024]{0:T(1024)} %param.20) | copy-start | bytes 12292
  158.8 4.7 %copy-start.3 = (s32[96,8]{0,1:T(8,128)S(1)}, s32[96,8]{0,1:T(8,128)}, u32[]{:S(2)}) copy-start(s32[96,8]{0,1:T(8,128)} %param.23) | copy-start | bytes 9220
  178.4 100.2 %copy-start.6 = (bf16[1,2048,768]{2,1,0:T(8,128)(2,1)S(1)}, bf16[1,2048,768]{2,1,0:T(8,128)(2,1)}, u32[]{:S(2)}) copy-start(bf16[1,2048,768]{2,1,0:T(8,128)(2,1)} %param.26) | copy-start | bytes 9437188
  276.7 2.0 copy-start.1
  296.1 97.8 %all-to-all-start.1 = ((bf16[16,64,2048]{2,1,0:T(8,128)(2,1)}), bf16[16,64,2048]{2,1,0:T(8,128)(2,1)}, u32[]{:S(2)}, u32[]{:S(2)}) async-start(bf16[16,64,2048]{2,1,0:T(8,128)(2,1)} %bitcast.113), calls=%async_computation.2 | async-start | bytes 8388608 | tf_op jit(solution)/shard_map/all_to_all | solution.py:117
Sparse Core Ops, SparseCore 0:
  11.7 72.1 all-gather.5
  86.0 72.7 all-gather.3
  163.6 11.0 reduce-scatter.1
where the time goes:
time: 417 us; the launch traced here: 416 us
  waiting for transfers between devices  196 us (47%)
  blocking collectives  111 us (27%)
  matrix products  34.3 us (8%)
  local copies, waits for them, and re-layouts  24.8 us (6%)
  other arithmetic  24.7 us (6%)
  between operations  13.9 us (3%)
  loops' own time  5.69 us (1%)
  starting transfers between devices  5.41 us (1%)
    all_to_all x1, blocking collectives, local(): lax.all_to_all(outgoing, ('seq', 'head'), split_axis=0, concat_axis=0, ti...  98.2 us
    all_to_all x1, waiting for transfers between devices, local(): lax.all_to_all(answer.reshape(row_shape), ('seq', 'head'), split_axis=0,...  84.9 us
    all_gather x1, waiting for transfers between devices, local(): lax.all_gather(out_proj, 'seq', axis=1, tiled=True)  53.9 us
    all_gather x1, waiting for transfers between devices, carried_in(): gathered = jax.tree.map(lambda a: lax.all_gather(a, axis), part)  50.6 us
    unnamed x1, blocking collectives  12.7 us
    dot_general x1, matrix products, local(): jnp.dot(inner, w_down[0], preferred_element_type=jnp.float32)  12.3 us
    gather x1, local copies, waits for them, and re-layouts, local(): jnp.take(flat_out, destination.reshape(-1), axis=0)  9.83 us
  transfers between devices with their start and end apart: 4, of which 4 were waited for; matrix products, arithmetic and copies ran while one was open for 8% of the time, Pallas kernels for 0%

commit v1 on v0

v1 whole, which is shorter than its diff:
```python
import jax
import jax.numpy as jnp
from jax import lax
from jax.sharding import PartitionSpec as P

D = 2048
DK = 128

epsilon = 1e-06


def local(
    queries,
    keys,
    values,
    segments,
    hidden_in,
    attn_gain,
    out_proj,
    moe_gain,
    route_ids,
    route_w,
    w_gate,
    w_up,
    w_down,
):
    tok_rows = queries.shape[0]
    heads_here = attn_gain.shape[0] // DK
    query_rows = queries.reshape(tok_rows, heads_here, DK)
    key_rows = keys.reshape(tok_rows, heads_here, DK)
    value_rows = values.reshape(tok_rows, heads_here, DK)
    position = jnp.arange(tok_rows)
    causal = position[:, None] >= position[None, :]
    same_doc = (segments[:, None] == segments[None, :]) & causal
    tail_mask = (segments == segments[-1])[:, None, None]
    tail_keys = jnp.where(tail_mask, key_rows, jnp.zeros_like(key_rows))
    own_state = jnp.einsum(
        "thd,the->hde", tail_keys, value_rows, preferred_element_type=jnp.float32
    ).astype(jnp.bfloat16)
    last_seg = jnp.broadcast_to(segments[-1].astype(jnp.bfloat16), (1, DK, DK))
    payload = jnp.concatenate([own_state, last_seg], axis=0)
    gathered = lax.all_gather(payload, "seq")
    before = jnp.arange(gathered.shape[0]) < lax.axis_index("seq")
    opened = gathered[:, heads_here, 0, 0] == segments[0].astype(jnp.bfloat16)
    keep = (before & opened)[:, None, None, None]
    prefix_state = jnp.sum(
        jnp.where(keep, gathered[:, :heads_here].astype(jnp.float32), 0.0), axis=0
    ).astype(jnp.bfloat16)
    scores = jnp.einsum("thd,shd->hts", query_rows, key_rows, preferred_element_type=jnp.float32)
    scores = jnp.where(same_doc[None], scores, 0.0).astype(jnp.bfloat16)
    local_part = jnp.einsum("hts,shd->thd", scores, value_rows, preferred_element_type=jnp.float32)
    continued = (segments == segments[0])[:, None, None]
    carried_part = jnp.einsum(
        "thd,hde->the", query_rows, prefix_state, preferred_element_type=jnp.float32
    )
    attn_raw = local_part + jnp.where(continued, carried_part, 0.0)
    mean_square = jnp.mean(attn_raw * attn_raw, axis=-1, keepdims=True)
    attended = attn_raw * lax.rsqrt(mean_square + epsilon) * attn_gain.reshape(heads_here, DK)
    attended = attended.astype(jnp.bfloat16).reshape(tok_rows, heads_here * DK)
    partial_out = jnp.dot(
        attended,
        lax.all_gather(out_proj, "seq", axis=1, tiled=True),
        preferred_element_type=jnp.float32,
    )
    attn_out = lax.psum_scatter(partial_out, "head", scatter_dimension=0, tiled=True)
    mid_wide = (hidden_in.astype(jnp.float32) + attn_out).astype(jnp.bfloat16).astype(jnp.float32)
    mid_square = jnp.mean(mid_wide * mid_wide, axis=-1, keepdims=True)
    normed = (mid_wide * lax.rsqrt(mid_square + epsilon) * moe_gain).astype(jnp.bfloat16)
    weights = route_w / jnp.sum(route_w, axis=1, keepdims=True)
    experts = lax.axis_size("seq") * lax.axis_size("head")
    labels = jnp.arange(experts, dtype=jnp.int32)
    dense = jnp.sum(
        jnp.where(route_ids[:, :, None] == labels[None, None, :], weights[:, :, None], 0.0), axis=1
    )
    everywhere = ("seq", "head")
    dense_all = lax.all_gather(dense, everywhere, axis=0, tiled=True)
    mine = lax.axis_index(everywhere)
    row_weight = jnp.sum(jnp.where(labels[None, :] == mine, dense_all, 0.0), axis=1, keepdims=True)
    rows_all = lax.all_gather(normed, everywhere, axis=0, tiled=True)
    gate_part = jnp.dot(rows_all, w_gate[0], preferred_element_type=jnp.float32)
    up_part = jnp.dot(rows_all, w_up[0], preferred_element_type=jnp.float32)
    inner = (jax.nn.silu(gate_part) * up_part).astype(jnp.bfloat16)
    answer = jnp.dot(inner, w_down[0], preferred_element_type=jnp.float32)
    answer = (answer * row_weight).astype(jnp.bfloat16)
    mixture = lax.psum_scatter(answer, everywhere, scatter_dimension=0, tiled=True)
    return (mid_wide + mixture.astype(jnp.float32)).astype(jnp.bfloat16)


def solution(mesh):
    return jax.shard_map(
        local,
        mesh=mesh,
        in_specs=(
            P(("dp", "seq"), "head"),
            P(("dp", "seq"), "head"),
            P(("dp", "seq"), "head"),
            P(("dp", "seq")),
            P(("dp", "seq", "head"), None),
            P("head"),
            P("head", "seq"),
            P(),
            P(("dp", "seq", "head"), None),
            P(("dp", "seq", "head"), None),
            P(("seq", "head"), None, None),
            P(("seq", "head"), None, None),
            P(("seq", "head"), None, None),
        ),
        out_specs=P(("dp", "seq", "head"), None),
        check_vma=False,
    )
```

time: 417 us -> 335 us (0.80)
  blocking collectives: 111 us -> 15.7 us
  waiting for transfers between devices: 196 us -> 254 us
  local copies, waits for them, and re-layouts: 24.8 us -> 5.38 us
  other arithmetic: 24.7 us -> 10.8 us
  loops' own time: 5.69 us -> 0 us
  starting transfers between devices: 5.41 us -> 0.17 us
    all_to_all x1 -> x0, blocking collectives: 98.2 us -> none  [local(): lax.all_to_all(outgoing, ('seq', 'head'), split_axis=0, concat_axis=0, ti...]
    all_to_all x1 -> x0, waiting for transfers between devices: 84.9 us -> none  [local(): lax.all_to_all(answer.reshape(row_shape), ('seq', 'head'), split_axis=0,...]
    reduce_scatter x0 -> x1, waiting for transfers between devices: none -> 83.9 us  [local(): lax.psum_scatter(answer, everywhere, scatter_dimension=0, tiled=True)]
    all_gather x1 -> x2, waiting for transfers between devices: 50.6 us -> 88.7 us  [the longest x1 45.7 us: local(): gathered = lax.all_gather(payload, 'seq')]
    all_gather x0 -> x1, blocking collectives: none -> 15.7 us  [local(): dense_all = lax.all_gather(dense, everywhere, axis=0, tiled=True)]
    all_gather x1, waiting for transfers between devices: 53.9 us -> 69.3 us  [local(): lax.all_gather(out_proj, 'seq', axis=1, tiled=True)]
    unnamed x1 -> x0, blocking collectives: 12.7 us -> none
    gather x1 -> x0, local copies, waits for them, and re-layouts: 9.83 us -> none  [local(): jnp.take(flat_out, destination.reshape(-1), axis=0)]
  transfers between devices with their start and end apart: 4 -> 5, of which waited for: 4 -> 5; matrix products, arithmetic and copies ran while one was open for 8% -> 4% of each run, Pallas kernels for 0% -> 0%
where the time goes in v1:
time: 335 us; the launch traced here: 333 us
  waiting for transfers between devices  254 us (76%)
  matrix products  32.2 us (10%)
  blocking collectives  15.7 us (5%)
  between operations  14.6 us (4%)
  other arithmetic  10.8 us (3%)
  local copies, waits for them, and re-layouts  5.38 us (2%)
    reduce_scatter x1, waiting for transfers between devices, local(): lax.psum_scatter(answer, everywhere, scatter_dimension=0, tiled=True)  83.9 us
    all_gather x1, waiting for transfers between devices, local(): lax.all_gather(out_proj, 'seq', axis=1, tiled=True)  69.3 us
    all_gather x1, waiting for transfers between devices, local(): gathered = lax.all_gather(payload, 'seq')  45.7 us
    all_gather x1, waiting for transfers between devices, local(): rows_all = lax.all_gather(normed, everywhere, axis=0, tiled=True)  43 us
    all_gather x1, blocking collectives, local(): dense_all = lax.all_gather(dense, everywhere, axis=0, tiled=True)  15.7 us
    reduce_scatter x1, waiting for transfers between devices, local(): lax.psum_scatter(partial_out, 'head', scatter_dimension=0, tiled=True)  11.2 us
    dot_general x1, matrix products, local(): gate_part = jnp.dot(rows_all, w_gate[0], preferred_element_type=jnp.float32)  8.21 us
    dot_general x1, matrix products, local(): answer = jnp.dot(inner, w_down[0], preferred_element_type=jnp.float32)  7.08 us
  transfers between devices with their start and end apart: 5, of which 5 were waited for; matrix products, arithmetic and copies ran while one was open for 4% of the time, Pallas kernels for 0%

profile of v1, /device:TPU:13, one launch (start us, length us, event | category | flops | bytes accessed | tf_op | source)
XLA Modules:
  0.0 332.5 jit_solution(12445706479404550765)
XLA Ops:
  6.5 0.0 copy-start
  6.5 0.0 copy-start.1
  6.5 0.0 all-gather.10.cloned.1.call-start
  6.5 1.4 fusion.39
  8.6 2.0 broadcast_compare_fusion
  10.6 1.5 convolution_convert_fusion
  12.1 0.7 concatenate.3
  12.9 0.0 all-gather.10.cloned.1.call-update
  12.9 0.0 all-gather.6.cloned.1.call-start
  13.0 0.7 all-gather.6.cloned.1.call-update
  13.7 0.0 reduce-scatter.3.cloned.1.call-start
  14.4 1.5 fusion.36
  15.8 2.8 fusion.5
  18.6 45.7 %all-gather.10.cloned.1.call-done = bf16[72,128,128]{2,1,0:T(8,128)(2,1)} async-done(((bf16[9,128,128]{2,1,0:T(8,128)(2,1)}), bf16[72,128,128]{2,1,0:T(8,128)(2,1)}) %all-gather.10.cloned.1.call-update) | async-done | bytes 2359312 | tf_op jit(solution)/shard_map/all_gather | solution.py:42
  64.3 0.7 slice.18
  65.0 0.1 copy.59
  65.1 2.1 select_reduce_fusion
  67.2 0.0 copy-done.1
  67.2 2.3 multiply_reduce_fusion
  69.5 69.3 %all-gather.6.cloned.1.call-done = bf16[1024,2048]{1,0:T(8,128)(2,1)} async-done(((bf16[1024,256]{1,0:T(8,128)(2,1)}), bf16[1024,2048]{1,0:T(8,128)(2,1)}) %all-gather.6.cloned.1.call-update) | async-done | bytes 4194320 | tf_op jit(solution)/shard_map/all_gather | solution.py:62
  138.8 0.0 copy-start.3
  138.8 0.0 copy-start.2
  138.8 0.0 copy-start.4
  138.8 4.7 %fusion.15 = f32[192,2048]{1,0:T(8,128)} fusion(bf16[1024,2048]{1,0:T(8,128)(2,1)} %all-gather.6.cloned.1.call-done, f32[192,8,128]{2,0,1:T(8,128)} %get-tuple-element.12, f32[8,128]{1,0:T(8,128)} %bitcast.81, f32[192,8]{0,1:T(8,128)S(1)} %add_rsqrt_fusion), kind=kOutput, calls=%fused_computation.27 | convolution fusion | flops 805896192 | bytes 6563840 | tf_op jit(solution)/shard_map/dot_general | solution.py:60
  143.5 0.0 reduce-scatter.3.cloned.1.call-update
  143.5 0.0 all-gather.8.cloned.1.call-start
  143.6 11.2 %reduce-scatter.3.cloned.1.call-done = f32[96,2048]{1,0:T(8,128)} async-done(((f32[192,2048]{1,0:T(8,128)}), f32[96,2048]{1,0:T(8,128)}) %reduce-scatter.3.cloned.1.call-update) | async-done | bytes 786448 | tf_op jit(solution)/shard_map/reduce_scatter | solution.py:65
  154.8 1.4 fusion.8
  156.2 0.0 copy-done.3
  156.2 0.9 fusion.10
  157.1 0.0 all-gather.8.cloned.1.call-update
  157.2 0.0 reduce-scatter.5.cloned.1.call-start
  157.2 0.0 copy-done.2
  157.3 0.0 copy-done.4
  157.3 15.7 %all-gather.1 = f32[16,96,16]{1,2,0:T(8,128)S(1)} all-gather(f32[1,96,16]{1,2,0:T(8,128)S(1)} %bitcast.80), channel_id=1, replica_groups=mesh['dp'=2,'seq'=8,'head'=2] {'seq','head'}, dimensions={0}, use_global_device_ids=true | all-gather | bytes 104448 | tf_op jit(solution)/shard_map/all_gather | solution.py:76
  173.0 0.7 copy.58
  173.7 1.7 reshape.94
  175.3 1.0 select_reduce_fusion.1
  176.3 43.0 %all-gather.8.cloned.1.call-done = bf16[1536,2048]{1,0:T(8,128)(2,1)} async-done(((bf16[96,2048]{1,0:T(8,128)(2,1)}), bf16[1536,2048]{1,0:T(8,128)(2,1)}) %all-gather.8.cloned.1.call-update) | async-done | bytes 6291472 | tf_op jit(solution)/shard_map/all_gather | solution.py:79
  219.3 0.0 copy-start.5
  219.3 0.0 copy-start.6
  219.3 8.2 %fusion.2 = f32[1536,768]{1,0:T(8,128)S(1)} fusion(bf16[1536,2048]{1,0:T(8,128)(2,1)} %all-gather.8.cloned.1.call-done, bf16[1,2048,768]{2,1,0:T(8,128)(2,1)} %param.23), kind=kOutput, calls=%fused_computation.5 | convolution fusion | flops 4831838208 | bytes 14155776 | tf_op jit(solution)/shard_map/dot_general | solution.py:80
  227.6 0.0 copy-done.5
  227.6 0.0 copy-done.6
  227.6 5.6 %multiply_convert_fusion.1 = bf16[1536,768]{1,0:T(8,128)(2,1)S(1)} fusion(f32[1536,768]{1,0:T(8,128)S(1)} %fusion.2, bf16[1536,2048]{1,0:T(8,128)(2,1)S(1)} %copy-done.5, bf16[1,2048,768]{2,1,0:T(8,128)(2,1)S(1)} %copy-done.6), kind=kOutput, calls=%fused_computation.1 | convolution fusion | flops 4838916096 | bytes 16515072 | tf_op jit(solution)/shard_map/dot_general | solution.py:81
  233.2 0.0 copy-done
  233.2 7.1 %multiply_convert_fusion = bf16[1536,2048]{1,0:T(8,128)(2,1)} fusion(bf16[1536,768]{1,0:T(8,128)(2,1)S(1)} %multiply_convert_fusion.1, f32[1536]{0:T(1024)S(1)} %select_reduce_fusion.1, bf16[1,768,2048]{2,1,0:T(8,128)(2,1)S(1)} %copy-done), kind=kOutput, calls=%fused_computation | convolution fusion | flops 4838129664 | bytes 11802624 | tf_op jit(solution)/shard_map/dot_general | solution.py:83
  240.3 0.0 reduce-scatter.5.cloned.1.call-update
  240.3 83.9 %reduce-scatter.5.cloned.1.call-done = bf16[96,2048]{1,0:T(8,128)(2,1)} async-done(((bf16[1536,2048]{1,0:T(8,128)(2,1)}), bf16[96,2048]{1,0:T(8,128)(2,1)}) %reduce-scatter.5.cloned.1.call-update) | async-done | bytes 393232 | tf_op jit(solution)/shard_map/reduce_scatter | solution.py:85
  324.2 1.8 fusion.11
  (7 shorter events, 0.1 us)
Async XLA Ops:
  6.5 226.7 %copy-start = (bf16[1,768,2048]{2,1,0:T(8,128)(2,1)S(1)}, bf16[1,768,2048]{2,1,0:T(8,128)(2,1)}, u32[]{:S(2)}) copy-start(bf16[1,768,2048]{2,1,0:T(8,128)(2,1)} %param.25) | copy-start | bytes 9437188
  6.5 60.6 %copy-start.1 = (bf16[192,1024]{1,0:T(8,128)(2,1)S(1)}, bf16[192,1024]{1,0:T(8,128)(2,1)}, u32[]{:S(2)}) copy-start(bf16[192,1024]{1,0:T(8,128)(2,1)} %param.13) | copy-start | bytes 1179652
  6.5 57.7 %all-gather.10.cloned.1.call-start = ((), (), s32[]{:S(2)}) async-start(), calls=%async_computation.6 | async-start | bytes 2654208 | tf_op jit(solution)/shard_map/all_gather | solution.py:42
  12.9 125.9 %all-gather.6.cloned.1.call-start = ((), (), s32[]{:S(2)}) async-start(), calls=%async_computation.2 | async-start | bytes 4718592 | tf_op jit(solution)/shard_map/all_gather | solution.py:62
  13.7 141.1 %reduce-scatter.3.cloned.1.call-start = ((), (), s32[]{:S(2)}) async-start(), calls=%async_computation.3 | async-start | bytes 2359296 | tf_op jit(solution)/shard_map/reduce_scatter | solution.py:65
  138.8 17.4 %copy-start.3 = (f32[2048]{0:T(1024)S(1)}, f32[2048]{0:T(1024)}, u32[]{:S(2)}) copy-start(f32[2048]{0:T(1024)} %param.20) | copy-start | bytes 24580
  138.8 18.4 %copy-start.2 = (f32[96,8]{0,1:T(8,128)S(1)}, f32[96,8]{0,1:T(8,128)}, u32[]{:S(2)}) copy-start(f32[96,8]{0,1:T(8,128)} %param.22) | copy-start | bytes 9220
  138.8 18.5 %copy-start.4 = (s32[96,8]{0,1:T(8,128)S(1)}, s32[96,8]{0,1:T(8,128)}, u32[]{:S(2)}) copy-start(s32[96,8]{0,1:T(8,128)} %param.21) | copy-start | bytes 9220
  143.5 75.8 %all-gather.8.cloned.1.call-start = ((), (), s32[]{:S(2)}) async-start(), calls=%async_computation.4 | async-start | bytes 6684672 | tf_op jit(solution)/shard_map/all_gather | solution.py:79
  157.2 167.0 %reduce-scatter.5.cloned.1.call-start = ((), (), s32[]{:S(2)}) async-start(), calls=%async_computation.5 | async-start | bytes 6684672 | tf_op jit(solution)/shard_map/reduce_scatter | solution.py:85
  219.3 8.2 %copy-start.5 = (bf16[1536,2048]{1,0:T(8,128)(2,1)S(1)}, bf16[1536,2048]{1,0:T(8,128)(2,1)}, u32[]{:S(2)}) copy-start(bf16[1536,2048]{1,0:T(8,128)(2,1)} %all-gather.8.cloned.1.call-done) | copy-start | bytes 18874372
  219.3 8.2 %copy-start.6 = (bf16[1,2048,768]{2,1,0:T(8,128)(2,1)S(1)}, bf16[1,2048,768]{2,1,0:T(8,128)(2,1)}, u32[]{:S(2)}) copy-start(bf16[1,2048,768]{2,1,0:T(8,128)(2,1)} %param.24) | copy-start | bytes 9437188
Sparse Core Ops, SparseCore 0:
  13.0 51.1 all-gather.9
  66.3 72.4 all-gather.5
  143.6 11.0 reduce-scatter.2
  157.3 62.0 all-gather.7
  240.4 83.7 reduce-scatter.4

commit v2 on v1

--- a/solution.py
+++ b/solution.py
@@ -1,12 +1,133 @@
+import functools
+
 import jax
 import jax.numpy as jnp
 from jax import lax
+from jax.experimental import pallas as pl
+from jax.experimental.pallas import tpu as pltpu
 from jax.sharding import PartitionSpec as P
 
 D = 2048
 DK = 128
 
 epsilon = 1e-06
+
+
+def gather_kernel(n_seq, cores, block, out, own_sem, send_sem, recv_sem):
+    place, core = lax.axis_index("seq"), lax.axis_index("head")
+    length = n_seq // 2
+    far, near = place // 2, place % 2
+    other = 1 - near
+
+    def slot(row, col, of):
+        return (row * 2 + col) * cores + (of if cores > 1 else 0)
+
+    def send(way, src, at, row, col, of):
+        return pltpu.make_async_remote_copy(
+            src_ref=src,
+            dst_ref=out.at[at],
+            send_sem=send_sem.at[way, at],
+            recv_sem=recv_sem.at[at],
+            device_id={"seq": row * 2 + col, "head": of},
+            device_id_type=pl.DeviceIdType.MESH,
+        )
+
+    def arrive(at):
+        send(0, out.at[at], at, far, other, core).wait_recv()
+
+    def up(src, at):
+        return send(0, src, at, far + 1, near, core)
+
+    def down(src, at):
+        return send(1, src, at, far - 1, near, core)
+
+    def across(src, at):
+        return send(2, src, at, far, other, core)
+
+    def beside(src, at):
+        return send(3, src, at, far, near, 1 - core)
+
+    barrier = pltpu.get_barrier_semaphore()
+
+    def greet(row, col, of):
+        pl.semaphore_signal(
+            barrier,
+            inc=1,
+            device_id={"seq": row * 2 + col, "head": of},
+            device_id_type=pl.DeviceIdType.MESH,
+        )
+
+    pl.when(far > 0)(lambda: greet(far - 1, near, core))
+    pl.when(far < length - 1)(lambda: greet(far + 1, near, core))
+    greet(far, other, core)
+    if cores > 1:
+        greet(far, near, 1 - core)
+    lines = jnp.where(far > 0, 1, 0) + jnp.where(far < length - 1, 1, 0)
+    pl.semaphore_wait(barrier, lines + (2 if cores > 1 else 1))
+
+    mine = slot(far, near, core)
+    pl.when(far < length - 1)(lambda: up(block, mine).start())
+    pl.when(far > 0)(lambda: down(block, mine).start())
+    across(block, mine).start()
+    if cores > 1:
+        beside(block, mine).start()
+    keep = pltpu.make_async_copy(block, out.at[mine], own_sem)
+    keep.start()
+
+    def from_line(row, onward, more):
+        at = slot(row, near, core)
+        arrive(at)
+        pl.when(more)(lambda: onward(out.at[at], at).start())
+        across(out.at[at], at).start()
+        if cores > 1:
+            beside(out.at[at], at).start()
+
+    def from_other(row):
+        at = slot(row, other, core)
+        arrive(at)
+        if cores > 1:
+            beside(out.at[at], at).start()
+
+    for step in range(1, length + 1):
+        if step < length:
+            pl.when(far - step >= 0)(lambda: from_line(far - step, up, far < length - 1))
+            pl.when(far + step < length)(lambda: from_line(far + step, down, far > 0))
+        if step == 1:
+            from_other(far)
+        else:
+            pl.when(far - step + 1 >= 0)(lambda: from_other(far - step + 1))
+            pl.when(far + step - 1 < length)(lambda: from_other(far + step - 1))
+    if cores > 1:
+        for row in range(length):
+            for col in range(2):
+                arrive(slot(row, col, 1 - core))
+    keep.wait()
+    for row in range(length):
+        at = slot(row, near, core)
+        pl.when((row <= far) & (far < length - 1))(lambda: up(out.at[at], at).wait_send())
+        pl.when((row >= far) & (far > 0))(lambda: down(out.at[at], at).wait_send())
+        across(out.at[at], at).wait_send()
+        if cores > 1:
+            beside(out.at[at], at).wait_send()
+            at = slot(row, other, core)
+            beside(out.at[at], at).wait_send()
+
+
+def gather(block, cores, ident):
+    n_seq = lax.axis_size("seq")
+    slots = n_seq * cores
+    return pl.pallas_call(
+        functools.partial(gather_kernel, n_seq, cores),
+        out_shape=jax.ShapeDtypeStruct((slots, *block.shape), block.dtype),
+        in_specs=[pl.BlockSpec(memory_space=pl.ANY)],
+        out_specs=pl.BlockSpec(memory_space=pl.ANY),
+        scratch_shapes=[
+            pltpu.SemaphoreType.DMA,
+            pltpu.SemaphoreType.DMA((4, slots)),
+            pltpu.SemaphoreType.DMA((slots,)),
+        ],
+        compiler_params=pltpu.CompilerParams(collective_id=ident, has_side_effects=True),
+    )(block)
 
 
 def local(
@@ -39,7 +160,7 @@
     ).astype(jnp.bfloat16)
     last_seg = jnp.broadcast_to(segments[-1].astype(jnp.bfloat16), (1, DK, DK))
     payload = jnp.concatenate([own_state, last_seg], axis=0)
-    gathered = lax.all_gather(payload, "seq")
+    gathered = gather(payload, 1, 0)
     before = jnp.arange(gathered.shape[0]) < lax.axis_index("seq")
     opened = gathered[:, heads_here, 0, 0] == segments[0].astype(jnp.bfloat16)
     keep = (before & opened)[:, None, None, None]
@@ -76,7 +197,7 @@
     dense_all = lax.all_gather(dense, everywhere, axis=0, tiled=True)
     mine = lax.axis_index(everywhere)
     row_weight = jnp.sum(jnp.where(labels[None, :] == mine, dense_all, 0.0), axis=1, keepdims=True)
-    rows_all = lax.all_gather(normed, everywhere, axis=0, tiled=True)
+    rows_all = gather(normed, lax.axis_size("head"), 1).reshape(-1, normed.shape[1])
     gate_part = jnp.dot(rows_all, w_gate[0], preferred_element_type=jnp.float32)
     up_part = jnp.dot(rows_all, w_up[0], preferred_element_type=jnp.float32)
     inner = (jax.nn.silu(gate_part) * up_part).astype(jnp.bfloat16)

time: 335 us -> 282 us (0.84)
  waiting for transfers between devices: 254 us -> 124 us
  Pallas kernels: 0 us -> 80.8 us
    all_gather x2 -> x0, waiting for transfers between devices: 88.7 us -> none  [the longest x1 45.7 us: local(): gathered = lax.all_gather(payload, 'seq')]
    pallas_call x0 -> x2, Pallas kernels: none -> 80.8 us  [gather(): pl.pallas_call(functools.partial(gather_kernel, n_seq, cores), out_shape=...]
    all_gather x1, waiting for transfers between devices: 69.3 us -> 37.1 us  [local(): lax.all_gather(out_proj, 'seq', axis=1, tiled=True)]
    reduce_scatter x1, waiting for transfers between devices: 11.2 us -> 0.02 us  [local(): lax.psum_scatter(partial_out, 'head', scatter_dimension=0, tiled=True)]
  transfers between devices with their start and end apart: 5 -> 3, of which waited for: 5 -> 2; matrix products, arithmetic and copies ran while one was open for 4% -> 5% of each run, Pallas kernels for 0% -> 13%
where the time goes in v2:
time: 282 us; the launch traced here: 280 us
  waiting for transfers between devices  124 us (44%)
  Pallas kernels  80.8 us (29%)
  matrix products  32.1 us (11%)
  blocking collectives  15.8 us (6%)
  between operations  14.6 us (5%)
  other arithmetic  10.2 us (4%)
    reduce_scatter x1, waiting for transfers between devices, local(): lax.psum_scatter(answer, everywhere, scatter_dimension=0, tiled=True)  86.1 us
    pallas_call x2, Pallas kernels, gather(): pl.pallas_call(functools.partial(gather_kernel, n_seq, cores), out_shape=...  80.8 us
    all_gather x1, waiting for transfers between devices, local(): lax.all_gather(out_proj, 'seq', axis=1, tiled=True)  37.1 us
    all_gather x1, blocking collectives, local(): dense_all = lax.all_gather(dense, everywhere, axis=0, tiled=True)  15.8 us
    dot_general x1, matrix products, local(): gate_part = jnp.dot(rows_all, w_gate[0], preferred_element_type=jnp.float32)  8.22 us
    dot_general x1, matrix products, local(): answer = jnp.dot(inner, w_down[0], preferred_element_type=jnp.float32)  7.1 us
  transfers between devices with their start and end apart: 3, of which 2 were waited for; matrix products, arithmetic and copies ran while one was open for 5% of the time, Pallas kernels for 13%

profile of v2, /device:TPU:13, one launch (start us, length us, event | category | flops | bytes accessed | tf_op | source)
XLA Modules:
  0.0 279.9 jit_solution(1274028337802346838)
XLA Ops:
  6.5 0.0 copy-start
  6.5 0.0 copy-start.3
  6.5 0.0 copy-start.2
  6.5 0.0 all-gather.3.cloned.1.call-start
  6.5 0.7 all-gather.3.cloned.1.call-update
  7.3 0.0 reduce-scatter.3.cloned.1.call-start
  7.3 1.4 fusion.39
  10.0 1.9 broadcast_compare_fusion
  11.9 1.5 convolution_convert_fusion
  13.5 0.7 concatenate.3.block
  14.2 37.2 %shard_map.127 = bf16[8,9,128,128]{3,2,1,0:T(8,128)(2,1)} custom-call(bf16[9,128,128]{2,1,0:T(8,128)(2,1)} %concatenate.3.block), custom_call_target="tpu_custom_call" | custom-call | tf_op jit(solution)/shard_map/pallas_call | solution.py:119
  51.4 0.0 copy-start.7
  51.4 1.0 and_reduce_fusion
  52.4 0.0 copy-done.3
  52.4 0.7 fusion.36
  53.1 0.0 copy-done.2
  53.1 2.6 fusion.5
  55.8 2.2 select_reduce_fusion
  57.9 2.3 multiply_reduce_fusion
  60.3 0.0 copy-start.4
  60.3 0.0 copy-start.6
  60.3 37.1 %all-gather.3.cloned.1.call-done = bf16[1024,2048]{1,0:T(8,128)(2,1)} async-done(((bf16[1024,256]{1,0:T(8,128)(2,1)}), bf16[1024,2048]{1,0:T(8,128)(2,1)}) %all-gather.3.cloned.1.call-update) | async-done | bytes 4194320 | tf_op jit(solution)/shard_map/all_gather | solution.py:183
  97.4 0.0 copy-done.7
  97.4 0.0 copy-start.5
  97.4 4.7 %fusion.15 = f32[192,2048]{1,0:T(8,128)} fusion(bf16[1024,2048]{1,0:T(8,128)(2,1)} %all-gather.3.cloned.1.call-done, f32[192,8,128]{2,0,1:T(8,128)} %get-tuple-element.12, f32[8,128]{1,0:T(8,128)S(1)} %bitcast.79, f32[192,8]{0,1:T(8,128)S(1)} %add_rsqrt_fusion), kind=kOutput, calls=%fused_computation.27 | convolution fusion | flops 805896192 | bytes 6563840 | tf_op jit(solution)/shard_map/dot_general | solution.py:181
  102.0 0.0 reduce-scatter.3.cloned.1.call-update
  102.1 0.0 reduce-scatter.5.cloned.1.call-start
  102.1 0.0 copy-done.4
  102.2 0.0 copy-done.6
  102.2 15.8 %all-gather = f32[16,96,16]{1,2,0:T(8,128)S(1)} all-gather(f32[1,96,16]{1,2,0:T(8,128)S(1)} %bitcast.78), channel_id=1, replica_groups=mesh['dp'=2,'seq'=8,'head'=2] {'seq','head'}, dimensions={0}, use_global_device_ids=true | all-gather | bytes 104448 | tf_op jit(solution)/shard_map/all_gather | solution.py:197
  118.1 0.1 reshape.97
  118.2 0.1 select_reduce_fusion.1
  118.3 0.0 reduce-scatter.3.cloned.1.call-done
  118.3 1.4 fusion.8
  119.8 0.0 copy-done.5
  119.8 0.9 fusion.10.block
  120.7 43.7 %shard_map.128 = bf16[16,96,2048]{2,1,0:T(8,128)(2,1)} custom-call(bf16[96,2048]{1,0:T(8,128)(2,1)} %fusion.10.block), custom_call_target="tpu_custom_call" | custom-call | tf_op jit(solution)/shard_map/pallas_call | solution.py:119
  164.4 0.0 copy-start.1
  164.4 0.0 copy-start.8
  164.4 8.2 %fusion.2 = f32[1536,768]{1,0:T(8,128)S(1)} fusion(bf16[1536,2048]{1,0:T(8,128)(2,1)} %bitcast.76, bf16[1,2048,768]{2,1,0:T(8,128)(2,1)} %param.23), kind=kOutput, calls=%fused_computation.5 | convolution fusion | flops 4831838208 | bytes 14155776 | tf_op jit(solution)/shard_map/dot_general | solution.py:201
  172.6 0.0 copy-done.1
  172.6 0.0 copy-done.8
  172.6 5.6 %multiply_convert_fusion.1 = bf16[1536,768]{1,0:T(8,128)(2,1)S(1)} fusion(f32[1536,768]{1,0:T(8,128)S(1)} %fusion.2, bf16[1536,2048]{1,0:T(8,128)(2,1)S(1)} %bitcast.77, bf16[1,2048,768]{2,1,0:T(8,128)(2,1)S(1)} %copy-done.8), kind=kOutput, calls=%fused_computation.1 | convolution fusion | flops 4838916096 | bytes 16515072 | tf_op jit(solution)/shard_map/dot_general | solution.py:202
  178.2 0.0 copy-done
  178.3 7.1 %multiply_convert_fusion = bf16[1536,2048]{1,0:T(8,128)(2,1)} fusion(bf16[1536,768]{1,0:T(8,128)(2,1)S(1)} %multiply_convert_fusion.1, f32[1536]{0:T(1024)S(1)} %select_reduce_fusion.1, bf16[1,768,2048]{2,1,0:T(8,128)(2,1)S(1)} %copy-done), kind=kOutput, calls=%fused_computation | convolution fusion | flops 4838129664 | bytes 11802624 | tf_op jit(solution)/shard_map/dot_general | solution.py:204
  185.4 0.0 reduce-scatter.5.cloned.1.call-update
  185.4 86.1 %reduce-scatter.5.cloned.1.call-done = bf16[96,2048]{1,0:T(8,128)(2,1)} async-done(((bf16[1536,2048]{1,0:T(8,128)(2,1)}), bf16[96,2048]{1,0:T(8,128)(2,1)}) %reduce-scatter.5.cloned.1.call-update) | async-done | bytes 393232 | tf_op jit(solution)/shard_map/reduce_scatter | solution.py:206
  271.5 1.8 fusion.11
  (7 shorter events, 0.1 us)
Async XLA Ops:
  6.5 171.7 %copy-start = (bf16[1,768,2048]{2,1,0:T(8,128)(2,1)S(1)}, bf16[1,768,2048]{2,1,0:T(8,128)(2,1)}, u32[]{:S(2)}) copy-start(bf16[1,768,2048]{2,1,0:T(8,128)(2,1)} %param.25) | copy-start | bytes 9437188
  6.5 45.9 %copy-start.3 = (s32[192]{0:T(256)S(1)}, s32[192]{0:T(256)}, u32[]{:S(2)}) copy-start(s32[192]{0:T(256)} %param.16) | copy-start | bytes 2308
  6.5 46.6 %copy-start.2 = (bf16[192,1024]{1,0:T(8,128)(2,1)S(1)}, bf16[192,1024]{1,0:T(8,128)(2,1)}, u32[]{:S(2)}) copy-start(bf16[192,1024]{1,0:T(8,128)(2,1)} %param.13) | copy-start | bytes 1179652
  6.5 90.8 %all-gather.3.cloned.1.call-start = ((), (), s32[]{:S(2)}) async-start(), calls=%async_computation.2 | async-start | bytes 4718592 | tf_op jit(solution)/shard_map/all_gather | solution.py:183
  7.3 111.0 %reduce-scatter.3.cloned.1.call-start = ((), (), s32[]{:S(2)}) async-start(), calls=%async_computation.3 | async-start | bytes 2359296 | tf_op jit(solution)/shard_map/reduce_scatter | solution.py:186
  51.4 46.0 %copy-start.7 = (f32[1024]{0:T(1024)S(1)}, f32[1024]{0:T(1024)}, u32[]{:S(2)}) copy-start(f32[1024]{0:T(1024)} %param.18) | copy-start | bytes 12292
  60.3 41.9 %copy-start.4 = (f32[96,8]{0,1:T(8,128)S(1)}, f32[96,8]{0,1:T(8,128)}, u32[]{:S(2)}) copy-start(f32[96,8]{0,1:T(8,128)} %param.22) | copy-start | bytes 9220
  60.3 41.9 %copy-start.6 = (s32[96,8]{0,1:T(8,128)S(1)}, s32[96,8]{0,1:T(8,128)}, u32[]{:S(2)}) copy-start(s32[96,8]{0,1:T(8,128)} %param.21) | copy-start | bytes 9220
  97.4 22.4 %copy-start.5 = (f32[2048]{0:T(1024)S(1)}, f32[2048]{0:T(1024)}, u32[]{:S(2)}) copy-start(f32[2048]{0:T(1024)} %param.20) | copy-start | bytes 24580
  102.1 169.4 %reduce-scatter.5.cloned.1.call-start = ((), (), s32[]{:S(2)}) async-start(), calls=%async_computation.4 | async-start | bytes 6684672 | tf_op jit(solution)/shard_map/reduce_scatter | solution.py:206
  164.4 8.3 %copy-start.1 = (bf16[16,96,2048]{2,1,0:T(8,128)(2,1)S(1)}, bf16[16,96,2048]{2,1,0:T(8,128)(2,1)}, u32[]{:S(2)}) copy-start(bf16[16,96,2048]{2,1,0:T(8,128)(2,1)} %shard_map.128) | copy-start | bytes 18874372
  164.4 8.3 %copy-start.8 = (bf16[1,2048,768]{2,1,0:T(8,128)(2,1)S(1)}, bf16[1,2048,768]{2,1,0:T(8,128)(2,1)}, u32[]{:S(2)}) copy-start(bf16[1,2048,768]{2,1,0:T(8,128)(2,1)} %param.24) | copy-start | bytes 9437188
Sparse Core Ops, SparseCore 0:
  9.4 87.9 all-gather.2
  102.2 9.4 reduce-scatter.2
  185.5 85.9 reduce-scatter.4

commit v3 on v2

--- a/solution.py
+++ b/solution.py
@@ -128,6 +128,154 @@
         ],
         compiler_params=pltpu.CompilerParams(collective_id=ident, has_side_effects=True),
     )(block)
+
+
+def scatter_kernel(n_seq, parts, out, own, besides, across, below, above, own_sem, send_sem, recv_sem):
+    place, core = lax.axis_index("seq"), lax.axis_index("head")
+    length = n_seq // 2
+    far, near = place // 2, place % 2
+    other = 1 - near
+    tall = parts.shape[1]
+    piece = 16
+
+    def far_first(visit):
+        for step in range(length - 1, 0, -1):
+            pl.when(far + step < length)(lambda: visit(far + step, 1))
+            pl.when(far - step >= 0)(lambda: visit(far - step, -1))
+        visit(far, 0)
+
+    def send(kind, src, dst, at, row, col, of):
+        return pltpu.make_async_remote_copy(
+            src_ref=src,
+            dst_ref=dst.at[at],
+            send_sem=send_sem.at[kind, at],
+            recv_sem=recv_sem.at[kind, at],
+            device_id={"seq": row * 2 + col, "head": of},
+            device_id_type=pl.DeviceIdType.MESH,
+        )
+
+    def to_core(row, col):
+        at = row * 2 + col
+        return send(0, parts.at[at * 2 + 1 - core], besides, at, far, near, 1 - core)
+
+    def to_near(row):
+        return send(1, besides.at[row * 2 + other], across, row, far, other, core)
+
+    def go_up(row):
+        return send(2, besides.at[row * 2 + near], below, row, far + 1, near, core)
+
+    def go_down(row):
+        return send(3, besides.at[row * 2 + near], above, row, far - 1, near, core)
+
+    def load(row, col):
+        at = row * 2 + col
+        return pltpu.make_async_copy(parts.at[at * 2 + core], own.at[at], own_sem.at[at])
+
+    def add(target, *terms):
+        @pl.loop(0, tall // piece)
+        def _(turn):
+            rows = pl.ds(pl.multiple_of(turn * piece, piece), piece)
+            total = target[rows, :].astype(jnp.float32)
+            for term in terms:
+                total = total + term[rows, :].astype(jnp.float32)
+            target[rows, :] = total.astype(target.dtype)
+
+    barrier = pltpu.get_barrier_semaphore()
+
+    def greet(row, col, of):
+        pl.semaphore_signal(
+            barrier,
+            inc=1,
+            device_id={"seq": row * 2 + col, "head": of},
+            device_id_type=pl.DeviceIdType.MESH,
+        )
+
+    pl.when(far > 0)(lambda: greet(far - 1, near, core))
+    pl.when(far < length - 1)(lambda: greet(far + 1, near, core))
+    greet(far, other, core)
+    greet(far, near, 1 - core)
+    lines = jnp.where(far > 0, 1, 0) + jnp.where(far < length - 1, 1, 0)
+    pl.semaphore_wait(barrier, lines + 2)
+
+    def begin(col):
+        def visit(row, side):
+            to_core(row, col).start()
+            load(row, col).start()
+
+        return visit
+
+    far_first(begin(other))
+    far_first(begin(near))
+
+    def first(row, side):
+        at = row * 2 + other
+        load(row, other).wait()
+        to_core(row, other).wait_recv()
+        add(besides.at[at], own.at[at])
+        to_near(row).start()
+
+    def second(row, side):
+        at = row * 2 + near
+        load(row, near).wait()
+        to_core(row, near).wait_recv()
+        to_near(row).wait_recv()
+        add(besides.at[at], own.at[at], across.at[row])
+        if side >= 0:
+
+            @pl.when(far > 0)
+            def _():
+                go_up(row).wait_recv()
+                add(besides.at[at], below.at[row])
+
+            if side > 0:
+                go_up(row).start()
+        if side <= 0:
+
+            @pl.when(far < length - 1)
+            def _():
+                go_down(row).wait_recv()
+                add(besides.at[at], above.at[row])
+
+            if side < 0:
+                go_down(row).start()
+
+    far_first(first)
+    far_first(second)
+    out[...] = besides[far * 2 + near]
+
+    def finish(row, side):
+        to_core(row, other).wait_send()
+        to_core(row, near).wait_send()
+        to_near(row).wait_send()
+        if side > 0:
+            go_up(row).wait_send()
+        if side < 0:
+            go_down(row).wait_send()
+
+    far_first(finish)
+
+
+def scatter_sum(parts, ident):
+    n_seq = lax.axis_size("seq")
+    slots, tall, wide = parts.shape
+    length = n_seq // 2
+    held = [(n_seq, tall, wide)] * 2 + [(length, tall, wide)] * 3
+    taken = sum(n for n, _, _ in held) * tall * wide * parts.dtype.itemsize
+    return pl.pallas_call(
+        functools.partial(scatter_kernel, n_seq),
+        out_shape=jax.ShapeDtypeStruct((tall, wide), parts.dtype),
+        in_specs=[pl.BlockSpec(memory_space=pl.ANY)],
+        out_specs=pl.BlockSpec(memory_space=pltpu.VMEM),
+        scratch_shapes=[pltpu.VMEM(shape, parts.dtype) for shape in held]
+        + [
+            pltpu.SemaphoreType.DMA((n_seq,)),
+            pltpu.SemaphoreType.DMA((4, n_seq)),
+            pltpu.SemaphoreType.DMA((4, n_seq)),
+        ],
+        compiler_params=pltpu.CompilerParams(
+            collective_id=ident, has_side_effects=True, vmem_limit_bytes=taken + (4 << 20)
+        ),
+    )(parts)
 
 
 def local(
@@ -203,7 +351,7 @@
     inner = (jax.nn.silu(gate_part) * up_part).astype(jnp.bfloat16)
     answer = jnp.dot(inner, w_down[0], preferred_element_type=jnp.float32)
     answer = (answer * row_weight).astype(jnp.bfloat16)
-    mixture = lax.psum_scatter(answer, everywhere, scatter_dimension=0, tiled=True)
+    mixture = scatter_sum(answer.reshape(experts, -1, D), 2)
     return (mid_wide + mixture.astype(jnp.float32)).astype(jnp.bfloat16)
 
 

time: 282 us -> 237 us (0.84)
  waiting for transfers between devices: 124 us -> 37.9 us
  Pallas kernels: 80.8 us -> 122 us
    reduce_scatter x1 -> x0, waiting for transfers between devices: 86.1 us -> none  [local(): lax.psum_scatter(answer, everywhere, scatter_dimension=0, tiled=True)]
    pallas_call x0 -> x1, Pallas kernels: none -> 41.1 us  [scatter_sum(): pl.pallas_call(functools.partial(scatter_kernel, n_seq), out_shape=jax.Sh...]
  transfers between devices with their start and end apart: 3 -> 2, of which waited for: 2 -> 1; matrix products, arithmetic and copies ran while one was open for 5% -> 6% of each run, Pallas kernels for 13% -> 16%
where the time goes in v3:
time: 237 us; the launch traced here: 232 us
  Pallas kernels  122 us (51%)
  waiting for transfers between devices  37.9 us (16%)
  matrix products  30.3 us (13%)
  blocking collectives  15.8 us (7%)
  between operations  14.9 us (6%)
  other arithmetic  9.17 us (4%)
    pallas_call x2, Pallas kernels, gather(): pl.pallas_call(functools.partial(gather_kernel, n_seq, cores), out_shape=...  80.9 us
    pallas_call x1, Pallas kernels, scatter_sum(): pl.pallas_call(functools.partial(scatter_kernel, n_seq), out_shape=jax.Sh...  41.1 us
    all_gather x1, waiting for transfers between devices, local(): lax.all_gather(out_proj, 'seq', axis=1, tiled=True)  37.1 us
    all_gather x1, blocking collectives, local(): dense_all = lax.all_gather(dense, everywhere, axis=0, tiled=True)  15.8 us
    dot_general x1, matrix products, local(): gate_part = jnp.dot(rows_all, w_gate[0], preferred_element_type=jnp.float32)  8.22 us
    dot_general x1, matrix products, local(): up_part = jnp.dot(rows_all, w_up[0], preferred_element_type=jnp.float32)  5.61 us
    dot_general x1, matrix products, local(): answer = jnp.dot(inner, w_down[0], preferred_element_type=jnp.float32)  5.37 us
  transfers between devices with their start and end apart: 2, of which 1 were waited for; matrix products, arithmetic and copies ran while one was open for 6% of the time, Pallas kernels for 16%

profile of v3, /device:TPU:13, one launch (start us, length us, event | category | flops | bytes accessed | tf_op | source)
XLA Modules:
  0.0 232.4 jit_solution(6579151558787500653)
XLA Ops:
  6.5 0.0 copy-start
  6.5 0.0 copy-start.3
  6.5 0.0 copy-start.2
  6.5 0.0 all-gather.3.cloned.1.call-start
  6.5 0.7 all-gather.3.cloned.1.call-update
  7.3 0.0 reduce-scatter.2.cloned.1.call-start
  7.3 1.4 fusion.39
  10.0 1.9 broadcast_compare_fusion
  11.9 1.5 convolution_convert_fusion
  13.5 0.7 concatenate.3.block
  14.2 37.2 %shard_map.127 = bf16[8,9,128,128]{3,2,1,0:T(8,128)(2,1)} custom-call(bf16[9,128,128]{2,1,0:T(8,128)(2,1)} %concatenate.3.block), custom_call_target="tpu_custom_call" | custom-call | tf_op jit(solution)/shard_map/pallas_call | solution.py:119
  51.4 0.0 copy-start.7
  51.4 1.0 and_reduce_fusion
  52.4 0.0 copy-done.3
  52.4 0.7 fusion.36
  53.1 0.0 copy-done.2
  53.1 2.6 %fusion.5 = f32[192,8,128]{2,0,1:T(8,128)} fusion(pred[192,192]{1,0:T(8,128)(4,1)} %fusion.36, bf16[192,1024]{1,0:T(8,128)(2,1)} %param.15, bf16[192,1024]{1,0:T(8,128)(2,1)} %param.14, bf16[192,1024]{1,0:T(8,128)(2,1)S(1)} %copy-done.2), kind=kOutput, calls=%fused_computation.9 | convolution fusion | flops 151584768 | bytes 2002944 | tf_op jit(solution)/shard_map/hts,shd->thd/dot_general | solution.py:320
  55.8 2.2 select_reduce_fusion
  57.9 2.3 multiply_reduce_fusion
  60.3 0.0 copy-start.4
  60.3 0.0 copy-start.6
  60.3 37.1 %all-gather.3.cloned.1.call-done = bf16[1024,2048]{1,0:T(8,128)(2,1)} async-done(((bf16[1024,256]{1,0:T(8,128)(2,1)}), bf16[1024,2048]{1,0:T(8,128)(2,1)}) %all-gather.3.cloned.1.call-update) | async-done | bytes 4194320 | tf_op jit(solution)/shard_map/all_gather | solution.py:331
  97.4 0.0 copy-done.7
  97.4 0.0 copy-start.5
  97.4 4.7 %fusion.15 = f32[192,2048]{1,0:T(8,128)} fusion(bf16[1024,2048]{1,0:T(8,128)(2,1)} %all-gather.3.cloned.1.call-done, f32[192,8,128]{2,0,1:T(8,128)} %get-tuple-element.12, f32[8,128]{1,0:T(8,128)S(1)} %bitcast.81, f32[192,8]{0,1:T(8,128)S(1)} %add_rsqrt_fusion), kind=kOutput, calls=%fused_computation.27 | convolution fusion | flops 805896192 | bytes 6563840 | tf_op jit(solution)/shard_map/dot_general | solution.py:329
  102.0 0.0 reduce-scatter.2.cloned.1.call-update
  102.1 0.0 copy-done.4
  102.1 0.0 copy-done.6
  102.1 15.8 %all-gather = f32[16,96,16]{1,2,0:T(8,128)S(1)} all-gather(f32[1,96,16]{1,2,0:T(8,128)S(1)} %bitcast.80), channel_id=1, replica_groups=mesh['dp'=2,'seq'=8,'head'=2] {'seq','head'}, dimensions={0}, use_global_device_ids=true | all-gather | bytes 104448 | tf_op jit(solution)/shard_map/all_gather | solution.py:345
  118.0 0.1 reshape.101
  118.1 0.1 select_reduce_fusion.1
  118.2 0.0 reduce-scatter.2.cloned.1.call-done
  118.3 1.4 fusion.8
  119.7 0.0 copy-done.5
  119.7 0.9 fusion.10.block
  120.7 43.7 %shard_map.128 = bf16[16,96,2048]{2,1,0:T(8,128)(2,1)} custom-call(bf16[96,2048]{1,0:T(8,128)(2,1)} %fusion.10.block), custom_call_target="tpu_custom_call" | custom-call | tf_op jit(solution)/shard_map/pallas_call | solution.py:119
  164.3 0.0 copy-start.1
  164.3 0.0 copy-start.8
  164.4 8.2 %fusion.2 = f32[1536,768]{1,0:T(8,128)S(1)} fusion(bf16[1536,2048]{1,0:T(8,128)(2,1)} %bitcast.78, bf16[1,2048,768]{2,1,0:T(8,128)(2,1)} %param.23), kind=kOutput, calls=%fused_computation.5 | convolution fusion | flops 4831838208 | bytes 14155776 | tf_op jit(solution)/shard_map/dot_general | solution.py:349
  172.6 0.0 copy-done.1
  172.6 0.0 copy-done.8
  172.6 5.6 %multiply_convert_fusion.1 = bf16[1536,768]{1,0:T(8,128)(2,1)S(1)} fusion(f32[1536,768]{1,0:T(8,128)S(1)} %fusion.2, bf16[1536,2048]{1,0:T(8,128)(2,1)S(1)} %bitcast.79, bf16[1,2048,768]{2,1,0:T(8,128)(2,1)S(1)} %copy-done.8), kind=kOutput, calls=%fused_computation.1 | convolution fusion | flops 4838916096 | bytes 16515072 | tf_op jit(solution)/shard_map/dot_general | solution.py:350
  178.2 0.0 copy-done
  178.2 5.4 %multiply_convert_fusion = bf16[1536,2048]{1,0:T(8,128)(2,1)S(1)} fusion(bf16[1536,768]{1,0:T(8,128)(2,1)S(1)} %multiply_convert_fusion.1, f32[1536]{0:T(1024)S(1)} %select_reduce_fusion.1, bf16[1,768,2048]{2,1,0:T(8,128)(2,1)S(1)} %copy-done), kind=kOutput, calls=%fused_computation | convolution fusion | flops 4838129664 | bytes 11802624 | tf_op jit(solution)/shard_map/dot_general | solution.py:352
  183.6 41.1 %shard_map.129 = bf16[96,2048]{1,0:T(8,128)(2,1)S(1)} custom-call(bf16[16,96,2048]{2,1,0:T(8,128)(2,1)S(1)} %bitcast.77), custom_call_target="tpu_custom_call" | custom-call | tf_op jit(solution)/shard_map/pallas_call | solution.py:264
  224.8 0.8 fusion.11
  (7 shorter events, 0.1 us)
Async XLA Ops:
  6.5 171.7 %copy-start = (bf16[1,768,2048]{2,1,0:T(8,128)(2,1)S(1)}, bf16[1,768,2048]{2,1,0:T(8,128)(2,1)}, u32[]{:S(2)}) copy-start(bf16[1,768,2048]{2,1,0:T(8,128)(2,1)} %param.25) | copy-start | bytes 9437188
  6.5 45.9 %copy-start.3 = (s32[192]{0:T(256)S(1)}, s32[192]{0:T(256)}, u32[]{:S(2)}) copy-start(s32[192]{0:T(256)} %param.16) | copy-start | bytes 2308
  6.5 46.6 %copy-start.2 = (bf16[192,1024]{1,0:T(8,128)(2,1)S(1)}, bf16[192,1024]{1,0:T(8,128)(2,1)}, u32[]{:S(2)}) copy-start(bf16[192,1024]{1,0:T(8,128)(2,1)} %param.13) | copy-start | bytes 1179652
  6.5 90.8 %all-gather.3.cloned.1.call-start = ((), (), s32[]{:S(2)}) async-start(), calls=%async_computation.1 | async-start | bytes 4718592 | tf_op jit(solution)/shard_map/all_gather | solution.py:331
  7.3 111.0 %reduce-scatter.2.cloned.1.call-start = ((), (), s32[]{:S(2)}) async-start(), calls=%async_computation.2 | async-start | bytes 2359296 | tf_op jit(solution)/shard_map/reduce_scatter | solution.py:334
  51.4 46.0 %copy-start.7 = (f32[1024]{0:T(1024)S(1)}, f32[1024]{0:T(1024)}, u32[]{:S(2)}) copy-start(f32[1024]{0:T(1024)} %param.18) | copy-start | bytes 12292
  60.3 41.8 %copy-start.4 = (f32[96,8]{0,1:T(8,128)S(1)}, f32[96,8]{0,1:T(8,128)}, u32[]{:S(2)}) copy-start(f32[96,8]{0,1:T(8,128)} %param.22) | copy-start | bytes 9220
  60.3 41.9 %copy-start.6 = (s32[96,8]{0,1:T(8,128)S(1)}, s32[96,8]{0,1:T(8,128)}, u32[]{:S(2)}) copy-start(s32[96,8]{0,1:T(8,128)} %param.21) | copy-start | bytes 9220
  97.4 22.3 %copy-start.5 = (f32[2048]{0:T(1024)S(1)}, f32[2048]{0:T(1024)}, u32[]{:S(2)}) copy-start(f32[2048]{0:T(1024)} %param.20) | copy-start | bytes 24580
  164.3 8.3 %copy-start.1 = (bf16[16,96,2048]{2,1,0:T(8,128)(2,1)S(1)}, bf16[16,96,2048]{2,1,0:T(8,128)(2,1)}, u32[]{:S(2)}) copy-start(bf16[16,96,2048]{2,1,0:T(8,128)(2,1)} %shard_map.128) | copy-start | bytes 18874372
  164.3 8.3 %copy-start.8 = (bf16[1,2048,768]{2,1,0:T(8,128)(2,1)S(1)}, bf16[1,2048,768]{2,1,0:T(8,128)(2,1)}, u32[]{:S(2)}) copy-start(bf16[1,2048,768]{2,1,0:T(8,128)(2,1)} %param.24) | copy-start | bytes 9437188
Sparse Core Ops, SparseCore 0:
  9.4 87.9 all-gather.2
  102.2 9.4 reduce-scatter.1
